TPU v7x, 512 devices: a whole 4x4x16 slice. The times are simulated.
512 devices in a mesh: cuts: 2 (over y_lo), dp: 16 (over z), row: 4 (over y_hi, core), col: 4 (over x).
Axes of the slice: x: 4, y: 4 (y_hi: 2, y_lo: 2; y = y_hi * 2 + y_lo), z: 16, core: 2. Of those that a mesh axis runs over, the one named last changes fastest.
Arguments:
- tokens: bfloat16 [32768, 4096], P(('cuts', 'dp'), 'row'), may hold values from -6 to 6
- cotangent: bfloat16 [32768, 4096], P(('cuts', 'dp'), 'col'), may hold values from -0.03125 to 0.03125
- norm_gain: float32 [4096], P('row'), may hold values from 0.5 to 6
- row_prev: float32 [4, 1024], P('row', 'dp'), may hold values from 0.02 to 0.5
- col_prev: float32 [4096], P('col'), may hold values from 0.002 to 0.05
Outputs:
- update: float32 [4, 1024, 4096], P('row', 'dp', 'col')
- row_moment: float32 [4, 1024], P('row', 'dp')
- col_moment: float32 [4096], P('col')
All inputs are finite; a program needn't handle non-finite values.
Results may differ from a plain program's by a relative error of at most 0.0004.
Values sent between devices are 32-bit elements; how exact they have to be, the bound alone decides.
A program may use at most 64 MiB of HBM per device.

v0:
```python
import jax
import jax.numpy as jnp
from jax import lax
from jax.sharding import PartitionSpec as P

D = 4096
F = 4096


decay_rate = 0.975
epsilon_one = 1e-30
clip_level = 1.0


def gradient_rows(inputs, cotangent, gains):
    product = lax.dot_general(
        inputs, cotangent, (((0,), (0,)), ((), ())), preferred_element_type=jnp.float32
    )
    return product * gains[:, None]


def adafactor_step(gradient, rows_prev, cols_prev, down_columns, all_total):
    squares = gradient * gradient
    row_sum = lax.psum(jnp.sum(squares, axis=1), "col")
    col_sum = down_columns(jnp.sum(squares, axis=0))
    row_moment = decay_rate * rows_prev + (1.0 - decay_rate) * (row_sum / F + epsilon_one)
    col_moment = decay_rate * cols_prev + (1.0 - decay_rate) * (col_sum / D + epsilon_one)
    factor = row_moment[:, None] * col_moment[None, :]
    raw_update = gradient / jnp.sqrt(factor)
    total_squares = all_total(jnp.sum(raw_update * raw_update))
    clip_scale = jnp.maximum(1.0, jnp.sqrt(total_squares / (D * F)) / clip_level)
    return (raw_update / clip_scale, row_moment, col_moment)


def body(tokens, cotangent, norm_gain, row_prev, col_prev):
    slice_part = lax.psum_scatter(
        gradient_rows(tokens, cotangent, norm_gain), "dp", scatter_dimension=0, tiled=True
    )
    gradient = lax.psum(slice_part, "cuts")
    update, row_moment, col_moment = adafactor_step(
        gradient,
        row_prev[0],
        col_prev,
        lambda values: lax.psum(values, ("dp", "row")),
        lambda values: lax.psum(values, ("dp", "row", "col")),
    )
    return (update[None], row_moment[None], col_moment)


def solution(mesh):
    return jax.shard_map(
        body,
        mesh=mesh,
        in_specs=(
            P(("cuts", "dp"), "row"),
            P(("cuts", "dp"), "col"),
            P("row"),
            P("row", "dp"),
            P("col"),
        ),
        out_specs=(P("row", "dp", "col"), P("row", "dp"), P("col")),
        check_vma=False,
    )
```

profile of v0, /device:TPU:1, one launch (start us, length us, event | category | flops | bytes accessed | tf_op | source)
XLA Modules:
  0.0 937.7 jit_solution(15512773143829418762)
XLA Ops:
  7.2 0.0 copy-start
  7.2 0.0 reduce-scatter.2.cloned.1.call-start
  7.2 1.5 copy-done
  8.8 5.9 convolution_multiply_fusion
  14.7 0.0 copy-start.4
  14.7 0.0 copy-start.2
  14.7 0.0 reduce-scatter.2.cloned.1.call-update
  14.7 0.0 all-reduce.2.cloned.1.call-start
  14.7 75.6 %reduce-scatter.2.cloned.1.call-done = f32[64,1024]{1,0:T(8,128)} async-done(((f32[1024,1024]{1,0:T(8,128)}), f32[64,1024]{1,0:T(8,128)}) %reduce-scatter.2.cloned.1.call-update) | async-done | bytes 262160 | tf_op jit(solution)/shard_map/reduce_scatter | solution.py:36
  90.3 0.0 all-reduce.2.cloned.1.call-update
  90.4 54.8 %all-reduce.2.cloned.1.call-done = f32[64,1024]{1,0:T(8,128)} async-done(((f32[64,1024]{1,0:T(8,128)}), f32[64,1024]{1,0:T(8,128)}) %all-reduce.2.cloned.1.call-update) | async-done | bytes 262160 | tf_op jit(solution)/shard_map/psum | solution.py:39
  145.1 1.1 multiply_reduce_fusion.2
  146.2 8.4 psum.29
  154.6 132.2 %psum.30 = f32[1024]{0:T(1024)S(1)} all-reduce(f32[1024]{0:T(1024)S(1)} %get-tuple-element.4), channel_id=1, replica_groups=mesh['cuts'=2,'dp'=16,'row'=4,'col'=4] {'dp','row'}, use_global_device_ids=true, to_apply=%region_5.0 | all-reduce | flops 1024 | bytes 8192 | tf_op jit(solution)/shard_map/psum | solution.py:44
  286.8 0.0 copy-done.4
  286.8 0.0 copy-done.2
  286.8 0.0 copy-start.3
  286.9 0.0 copy-start.1
  286.9 1.7 multiply_reduce_fusion
  288.6 639.8 %psum.31 = f32[]{:T(128)} all-reduce(f32[]{:T(128)} %multiply_reduce_fusion), channel_id=1, replica_groups=mesh['cuts'=2,'dp'=16,'row'=4,'col'=4] {'dp','row','col'}, use_global_device_ids=true, to_apply=%region_7.0 | all-reduce | flops 1 | bytes 8 | tf_op jit(solution)/shard_map/psum | solution.py:45
  929.1 1.8 divide_bitcast_fusion
  930.8 0.0 copy-done.3
  930.8 0.0 copy-done.1
  (2 shorter events, 0.0 us)
Async XLA Ops:
  7.2 1.6 copy-start
  7.2 83.2 %reduce-scatter.2.cloned.1.call-start = ((), (), s32[]{:S(2)}) async-start(), calls=%async_computation.1 | async-start | bytes 4456448 | tf_op jit(solution)/shard_map/reduce_scatter | solution.py:36
  14.7 272.2 %copy-start.4 = (f32[1,64]{1,0:T(1,128)S(1)}, f32[1,64]{1,0:T(1,128)}, u32[]{:S(2)}) copy-start(f32[1,64]{1,0:T(1,128)} %param.8) | copy-start | bytes 772
  14.7 272.2 %copy-start.2 = (f32[1024]{0:T(1024)S(1)}, f32[1024]{0:T(1024)}, u32[]{:S(2)}) copy-start(f32[1024]{0:T(1024)} %param.9) | copy-start | bytes 12292
  14.7 130.4 %all-reduce.2.cloned.1.call-start = ((), (), s32[]{:S(2)}) async-start(), calls=%async_computation.2 | async-start | bytes 524288 | tf_op jit(solution)/shard_map/psum | solution.py:39
  286.8 644.0 %copy-start.3 = (f32[64]{0:T(128)}, f32[64]{0:T(128)S(1)}, u32[]{:S(2)}) copy-start(f32[64]{0:T(128)S(1)} %bitcast_add_fusion) | copy-start | bytes 772
  286.9 644.0 %copy-start.1 = (f32[1024]{0:T(1024)}, f32[1024]{0:T(1024)S(1)}, u32[]{:S(2)}) copy-start(f32[1024]{0:T(1024)S(1)} %multiply_add_fusion) | copy-start | bytes 12292
Sparse Core Ops, SparseCore 0:
  14.8 75.4 reduce-scatter.1
  93.2 51.8 all-reduce.1
where the time goes:
time: 947 us; the launch traced here: 938 us
  blocking collectives  780 us (82%)
  waiting for transfers between devices  130 us (14%)
  between operations  14.8 us (2%)
    psum x1, blocking collectives, body(): lax.psum(values, ('dp', 'row', 'col'))  640 us
    psum x1, blocking collectives, body(): lax.psum(values, ('dp', 'row'))  132 us
    reduce_scatter x1, waiting for transfers between devices, body(): lax.psum_scatter(gradient_rows(tokens, cotangent, norm_gain), 'dp', scatt...  75.6 us
    psum x1, waiting for transfers between devices, body(): gradient = lax.psum(slice_part, 'cuts')  54.8 us
  transfers between devices with their start and end apart: 2, of which 2 were waited for; matrix products, arithmetic and copies ran while one was open for 0% of the time, Pallas kernels for 0%

commit v1 on v0

v1 whole, which is shorter than its diff:
```python
import jax
import jax.numpy as jnp
from jax import lax
from jax.experimental import pallas as pl
from jax.experimental.pallas import tpu as pltpu
from jax.sharding import PartitionSpec as P

MESH = pl.DeviceIdType.MESH
F32 = jnp.float32

D = 4096
F = 4096
DECAY = 0.975
EPS = 1e-30
CLIP = 1.0

NZ, NROW, NCOL, NCUT = 16, 4, 4, 2
N8 = NROW * NCUT
ROWS = 64
HALF = 32
WIDE = 1024
W = 256
ZF = 2 * W

Z_CHUNKS = [(0, 1, 0), (W, 1, 1), (0, 0, 0), (W, 0, 1)]
Y_CHUNKS = [(ZF, 0, 0), (ZF + W, 0, 1)]
CHUNKS = Z_CHUNKS + Y_CHUNKS
NCH = len(CHUNKS)


def kernel(
    x_hbm, c_hbm, gain_ref, rprev_ref, cprev_ref,
    upd_ref, rmom_ref, cmom_ref,
    x_ref, c_ref, part, rbuf, ybuf, zx_src, zx_dst, gfull,
    rr, rx_src, rx_dst, ab_src, ab, zab, fin,
    in_sem, ssem, rsem, ys, yr, zxs, zxr, gs, gr, rs, rrs, rxs, rxr, abs_, abr, zs, zr, fs, fr,
):
    d = lax.axis_index("dp")
    c = lax.axis_index("cuts")
    row = lax.axis_index("row")
    col = lax.axis_index("col")
    other = 1 - c
    me8 = row * NCUT + c
    me32 = col * N8 + me8
    up = {"dp": lax.rem(d + 1, NZ)}
    down = {"dp": lax.rem(d + NZ - 1, NZ)}
    pair = {"cuts": other}

    def peer8(k):
        e = lax.rem(me8 + k, N8)
        return e, {"row": e // NCUT, "cuts": lax.rem(e, NCUT)}

    def remote(src, dst, s, r, dev):
        return pltpu.make_async_remote_copy(
            src_ref=src, dst_ref=dst, send_sem=s, recv_sem=r,
            device_id=dev, device_id_type=MESH,
        )

    load_c = pltpu.make_async_copy(c_hbm, c_ref, in_sem.at[0])
    load_x = pltpu.make_async_copy(x_hbm, x_ref, in_sem.at[1])
    load_c.start()
    load_x.start()

    barrier = pltpu.get_barrier_semaphore()

    def greet(dev):
        pl.semaphore_signal(barrier, inc=1, device_id=dev, device_id_type=MESH)

    greet(up)
    greet(down)
    for k in range(1, N8):
        greet(peer8(k)[1])
    for k in range(1, NCOL):
        greet({"col": lax.rem(col + k, NCOL)})

    load_c.wait()
    load_x.wait()

    def product(j):
        half = (j + 1) // 2
        step = jnp.where(j % 2 == 1, half, -half)
        p = lax.rem(d // 2 + 4 + step + 8, 8)
        at = pl.ds(pl.multiple_of(p * 128, 128), 128)
        part[at, :] = lax.dot_general(
            x_ref[:, at], c_ref[...], (((0,), (0,)), ((), ())),
            preferred_element_type=F32,
        )
        return p

    def y_copy(e):
        rows_ = pl.ds(pl.multiple_of(e * ROWS + other * HALF, HALF), HALF)
        return remote(part.at[rows_, pl.ds(ZF, WIDE - ZF)], ybuf.at[e], ys.at[e], yr.at[e], pair)

    def y_send(j):
        half = (j + 1) // 2
        step = jnp.where(j % 2 == 1, half, -half)
        p = lax.rem(d // 2 + 4 + step + 8, 8)
        y_copy(2 * p).start()
        y_copy(2 * p + 1).start()

    def first(j, _):
        product(j)
        return 0

    def later(j, _):
        product(j)
        y_send(j)
        return 0

    lax.fori_loop(0, 3, first, 0)
    pl.semaphore_wait(barrier, 2 + (N8 - 1) + (NCOL - 1))

    def reach(direction, which):
        return 8 if direction == which else 7

    def own(e, chunk):
        start, theirs, _ = chunk
        h = other if theirs else c
        return part.at[
            pl.ds(pl.multiple_of(e * ROWS + h * HALF, HALF), HALF), pl.ds(start, W)
        ]

    def dest(direction, distance):
        if direction == 0:
            return lax.rem(d + distance, NZ)
        return lax.rem(d + NZ - distance, NZ)

    def hop(direction, n, i, src):
        ch = direction * NCH + n
        return remote(
            src, rbuf.at[ch, i], ssem.at[ch, i], rsem.at[ch, i], down if direction else up
        )

    def begin(direction, n, i):
        hop(direction, n, i, own(dest(direction, 8 - i), CHUNKS[n])).start()

    def forward(direction, n, i):
        ch = direction * NCH + n
        slot = rbuf.at[ch, i - 1]
        hop(direction, n, i - 1, slot).wait_recv()
        slot[...] += own(dest(direction, 8 - i), CHUNKS[n])[...]
        hop(direction, n, i, slot).start()

    def y_add(e):
        y_copy(e).wait_recv()
        rows_ = pl.ds(pl.multiple_of(e * ROWS + c * HALF, HALF), HALF)
        part[rows_, pl.ds(ZF, WIDE - ZF)] += ybuf[e]

    zn = range(len(Z_CHUNKS))
    yn = range(len(Z_CHUNKS), NCH)

    for n in zn:
        which = CHUNKS[n][2]
        begin(which, n, 0)
    for j in range(3):
        y_send(j)
    for n in zn:
        which = CHUNKS[n][2]
        begin(1 - which, n, 1)
    lax.fori_loop(3, 8, later, 0)

    def z_first(i):
        for n in zn:
            which = CHUNKS[n][2]
            forward(which, n, i)

    def z_step(i):
        for n in zn:
            for direction in (0, 1):
                forward(direction, n, i)

    def y_step(i):
        y_add(dest(0, 8 - i))
        y_add(dest(1, 8 - i))
        for n in yn:
            for direction in (0, 1):
                forward(direction, n, i)

    z_first(1)
    y_add(dest(0, 8))
    for n in yn:
        begin(CHUNKS[n][2], n, 0)
    y_add(dest(0, 7))
    y_add(dest(1, 7))
    for n in yn:
        begin(1 - CHUNKS[n][2], n, 1)
    for n in yn:
        forward(CHUNKS[n][2], n, 1)

    def steps(i, _):
        z_step(i)
        y_step(i)
        return 0

    lax.fori_loop(2, 8, steps, 0)

    lane = lax.broadcasted_iota(jnp.int32, (HALF, WIDE), 1)
    sub = lax.broadcasted_iota(jnp.int32, (HALF, WIDE), 0)
    gain = jnp.sum(
        jnp.where(lane == sub + d * ROWS + c * HALF, gain_ref[...], 0.0), axis=1, keepdims=True
    )

    def collect(n):
        for direction in (0, 1):
            hop(direction, n, 7, rbuf.at[direction * NCH + n, 7]).wait_recv()
        return own(d, CHUNKS[n])[...] + rbuf[n, 7] + rbuf[NCH + n, 7]

    for n in zn:
        start, theirs, _ = CHUNKS[n]
        if theirs:
            zx_src[:, pl.ds(start, W)] = collect(n)
    zx = remote(zx_src, zx_dst, zxs, zxr, pair)
    zx.start()
    y_add(d)
    mine = pl.ds(pl.multiple_of(c * HALF, HALF), HALF)
    for n in range(NCH):
        start, theirs, _ = CHUNKS[n]
        if not theirs:
            gfull[mine, pl.ds(start, W)] = collect(n)
    zx.wait_recv()
    gfull[mine, pl.ds(0, ZF)] += zx_dst[...]
    g = gfull[mine, :] * gain
    gfull[mine, :] = g
    g_copy = remote(gfull.at[mine], gfull.at[mine], gs, gr, pair)
    g_copy.start()

    lane1 = lax.broadcasted_iota(jnp.int32, (HALF, 128), 1)
    sub1 = lax.broadcasted_iota(jnp.int32, (HALF, 128), 0)
    diag = lane1 == sub1 + c * HALF
    sq = g * g
    rsum = jnp.sum(sq, axis=1, keepdims=True)
    rr[col] = jnp.sum(jnp.where(diag, rsum, 0.0), axis=0, keepdims=True)
    rcopies = []
    for k in range(1, NCOL):
        to = lax.rem(col + k, NCOL)
        cp = remote(rr.at[col], rr.at[col], rs.at[k], rrs.at[col], {"col": to})
        cp.start()
        rcopies.append(cp)
    asum = jnp.sum(sq, axis=0, keepdims=True)
    for e in range(N8):
        ab_src[e, :, pl.ds(0, 128)] = asum[:, e * 128:(e + 1) * 128]
    for k in range(1, NCOL):
        frm = lax.rem(col + k, NCOL)
        remote(rr.at[frm], rr.at[frm], rs.at[k], rrs.at[frm], {"col": frm}).wait_recv()
    total = rr[0] + rr[1] + rr[2] + rr[3]
    lane_r = lax.broadcasted_iota(jnp.int32, (1, 128), 1)
    in_half = (lane_r >= c * HALF) & (lane_r < c * HALF + HALF)
    rprev = jnp.concatenate([rprev_ref[...], rprev_ref[...]], axis=1)
    rmom = DECAY * rprev + (1.0 - DECAY) * (total / F + EPS)
    rmom = jnp.where(in_half, rmom, 0.0)
    rx_src[...] = rmom
    rx = remote(rx_src, rx_dst, rxs, rxr, pair)
    rx.start()
    rcol = jnp.sum(jnp.where(diag, rmom, 0.0), axis=1, keepdims=True)
    bsum = jnp.sum(sq * (1.0 / rcol), axis=0, keepdims=True)
    for e in range(N8):
        ab_src[e, :, pl.ds(128, 128)] = bsum[:, e * 128:(e + 1) * 128]

    acopies = []
    for k in range(1, N8):
        e, dev = peer8(k)
        cp = remote(ab_src.at[e], ab.at[me8], abs_.at[k], abr.at[me8], dev)
        cp.start()
        acopies.append(cp)
    ab[me8] = ab_src[me8]
    for k in range(1, N8):
        e, dev = peer8(k)
        remote(ab_src.at[e], ab.at[e], abs_.at[k], abr.at[e], dev).wait_recv()
    acc = ab[0]
    for e in range(1, N8):
        acc = acc + ab[e]

    zab[d] = acc
    zcopies = []
    for k in range(1, NZ):
        to = lax.rem(d + k, NZ)
        cp = remote(zab.at[d], zab.at[d], zs.at[k], zr.at[d], {"dp": to})
        cp.start()
        zcopies.append(cp)
    cprev = cprev_ref[:, pl.ds(pl.multiple_of(me8 * 128, 128), 128)]
    for k in range(1, NZ):
        frm = lax.rem(d + k, NZ)
        remote(zab.at[frm], zab.at[frm], zs.at[k], zr.at[frm], {"dp": frm}).wait_recv()
    acc = zab[0]
    for e in range(1, NZ):
        acc = acc + zab[e]
    cmom = DECAY * cprev + (1.0 - DECAY) * (acc[:, 0:128] / D + EPS)
    fin[me32, :, pl.ds(0, 128)] = cmom
    fin[me32, :, pl.ds(128, 128)] = acc[:, 128:256] / cmom

    def plane(k):
        e = lax.rem(me32 + k, NCOL * N8)
        return e, {
            "col": e // N8,
            "row": lax.rem(e, N8) // NCUT,
            "cuts": lax.rem(e, NCUT),
        }

    fcopies = []
    for k in range(1, NCOL * N8):
        _, dev = plane(k)
        cp = remote(fin.at[me32], fin.at[me32], fs.at[k], fr.at[me32], dev)
        cp.start()
        fcopies.append(cp)

    rx.wait_recv()
    rfull = rmom + rx_dst[...]
    rmom_ref[...] = rfull[:, 0:ROWS]
    lane2 = lax.broadcasted_iota(jnp.int32, (ROWS, 128), 1)
    sub2 = lax.broadcasted_iota(jnp.int32, (ROWS, 128), 0)
    rscale = lax.rsqrt(jnp.sum(jnp.where(lane2 == sub2, rfull, 0.0), axis=1, keepdims=True))
    g_copy.wait_recv()

    for k in range(1, NCOL * N8):
        e, dev = plane(k)
        remote(fin.at[e], fin.at[e], fs.at[k], fr.at[e], dev).wait_recv()
    tot = fin[0, :, pl.ds(128, 128)]
    for e in range(1, NCOL * N8):
        tot = tot + fin[e, :, pl.ds(128, 128)]
    ratio = jnp.sum(tot, axis=1, keepdims=True) / (D * F)
    inverse = 1.0 / jnp.maximum(1.0, jnp.sqrt(ratio) / CLIP)
    rows_scale = rscale * inverse
    for e in range(N8):
        at = pl.ds(e * 128, 128)
        cm = fin[col * N8 + e, :, pl.ds(0, 128)]
        cmom_ref[:, at] = cm
        upd_ref[:, at] = gfull[:, at] * rows_scale * lax.rsqrt(cm)

    for n in range(NCH):
        for direction in (0, 1):
            ch = direction * NCH + n
            lo = 0 if direction == CHUNKS[n][2] else 1

            def drain(i, _, direction=direction, n=n, ch=ch):
                hop(direction, n, i, rbuf.at[ch, i]).wait_send()
                return 0

            lax.fori_loop(lo, 8, drain, 0)

    def drain_y(e, _):
        y_copy(e).wait_send()
        return 0

    lax.fori_loop(0, NZ, drain_y, 0)
    zx.wait_send()
    g_copy.wait_send()
    rx.wait_send()
    for cp in rcopies + acopies + zcopies + fcopies:
        cp.wait_send()


def body(tokens, cotangent, norm_gain, row_prev, col_prev):
    vmem = pl.BlockSpec(memory_space=pltpu.VMEM)
    hbm = pl.BlockSpec(memory_space=pl.ANY)
    dma = pltpu.SemaphoreType.DMA
    update, row_moment, col_moment = pl.pallas_call(
        kernel,
        out_shape=(
            jax.ShapeDtypeStruct((ROWS, WIDE), F32),
            jax.ShapeDtypeStruct((1, ROWS), F32),
            jax.ShapeDtypeStruct((1, WIDE), F32),
        ),
        in_specs=[hbm, hbm, vmem, vmem, vmem],
        out_specs=(vmem, vmem, vmem),
        scratch_shapes=[
            pltpu.VMEM((1024, 1024), jnp.bfloat16),
            pltpu.VMEM((1024, 1024), jnp.bfloat16),
            pltpu.VMEM((1024, WIDE), F32),
            pltpu.VMEM((2 * NCH, 8, HALF, W), F32),
            pltpu.VMEM((NZ, HALF, WIDE - ZF), F32),
            pltpu.VMEM((HALF, ZF), F32),
            pltpu.VMEM((HALF, ZF), F32),
            pltpu.VMEM((ROWS, WIDE), F32),
            pltpu.VMEM((NCOL, 1, 128), F32),
            pltpu.VMEM((1, 128), F32),
            pltpu.VMEM((1, 128), F32),
            pltpu.VMEM((N8, 1, 256), F32),
            pltpu.VMEM((N8, 1, 256), F32),
            pltpu.VMEM((NZ, 1, 256), F32),
            pltpu.VMEM((NCOL * N8, 1, 256), F32),
            dma((2,)),
            dma((2 * NCH, 8)), dma((2 * NCH, 8)),
            dma((NZ,)), dma((NZ,)),
            dma, dma, dma, dma,
            dma((NCOL,)), dma((NCOL,)),
            dma, dma,
            dma((N8,)), dma((N8,)),
            dma((NZ,)), dma((NZ,)),
            dma((NCOL * N8,)), dma((NCOL * N8,)),
        ],
        compiler_params=pltpu.CompilerParams(
            collective_id=0, has_side_effects=True, vmem_limit_bytes=40 << 20
        ),
        name="adafactor",
    )(tokens, cotangent, norm_gain[None, :], row_prev, col_prev[None, :])
    return update[None], row_moment, col_moment[0]


def solution(mesh):
    return jax.shard_map(
        body,
        mesh=mesh,
        in_specs=(
            P(("cuts", "dp"), "row"),
            P(("cuts", "dp"), "col"),
            P("row"),
            P("row", "dp"),
            P("col"),
        ),
        out_specs=(P("row", "dp", "col"), P("row", "dp"), P("col")),
        check_vma=False,
    )
```

time: 947 us -> 85.9 us (0.09)
  blocking collectives: 780 us -> 0 us
  waiting for transfers between devices: 130 us -> 0 us
  Pallas kernels: 0 us -> 78 us
  between operations: 14.8 us -> 0.65 us
    psum x3 -> x0, blocking collectives: 780 us -> none  [the longest x1 640 us: body(): lax.psum(values, ('dp', 'row', 'col'))]
    pallas_call x0 -> x1, Pallas kernels: none -> 78 us  [body(): pl.pallas_call(kernel, out_shape=(jax.ShapeDtypeStruct((ROWS, WIDE), F32)...]
    reduce_scatter x1 -> x0, waiting for transfers between devices: 75.6 us -> none  [body(): lax.psum_scatter(gradient_rows(tokens, cotangent, norm_gain), 'dp', scatt...]
    psum x1 -> x0, waiting for transfers between devices: 54.8 us -> none  [body(): gradient = lax.psum(slice_part, 'cuts')]
  transfers between devices with their start and end apart: 2 -> 0, of which waited for: 2 -> 0; matrix products, arithmetic and copies ran while one was open for 0% -> 0% of each run, Pallas kernels for 0% -> 0%
where the time goes in v1:
time: 85.9 us; the launch traced here: 85.7 us
  Pallas kernels  78 us (91%)
  local copies, waits for them, and re-layouts  7.01 us (8%)
    pallas_call x1, Pallas kernels, body(): pl.pallas_call(kernel, out_shape=(jax.ShapeDtypeStruct((ROWS, WIDE), F32)...  78 us
    unnamed x13, local copies, waits for them, and re-layouts  7.01 us

profile of v1, /device:TPU:1, one launch (start us, length us, event | category | flops | bytes accessed | tf_op | source)
XLA Modules:
  0.0 85.7 jit_solution(13205310674378769113)
XLA Ops:
  0.6 0.0 copy-start
  0.6 1.6 %copy-done = bf16[1024,1024]{1,0:T(8,128)(2,1)S(1)} copy-done((bf16[1024,1024]{1,0:T(8,128)(2,1)S(1)}, bf16[1024,1024]{1,0:T(8,128)(2,1)}, u32[]{:S(2)}) %copy-start) | copy-done | bytes 2097176
  2.2 0.0 copy-start.1
  2.2 1.6 %copy-done.1 = bf16[1024,1024]{1,0:T(8,128)(2,1)S(1)} copy-done((bf16[1024,1024]{1,0:T(8,128)(2,1)S(1)}, bf16[1024,1024]{1,0:T(8,128)(2,1)}, u32[]{:S(2)}) %copy-start.1) | copy-done | bytes 2097176
  3.8 0.0 copy-start.2
  3.8 0.7 copy-done.2
  4.5 0.0 copy-start.3
  4.5 0.7 copy-done.3
  5.2 0.0 copy-start.4
  5.2 0.7 copy-done.4
  5.8 78.0 %adafactor.1 = (f32[64,1024]{1,0:T(8,128)S(1)}, f32[1,64]{1,0:T(1,128)S(1)}, f32[1,1024]{1,0:T(1,128)S(1)}) custom-call(bf16[1024,1024]{1,0:T(8,128)(2,1)S(1)} %copy-done, bf16[1024,1024]{1,0:T(8,128)(2,1)S(1)} %copy-done.1, f32[1,1024]{1,0:T(1,128)S(1)} %bitcast.6, f32[1,64]{1,0:T(1,128)S(1)} %copy-done.4, f32[1,1024]{1,0:T(1,128)S(1)} %bitcast.7), custom_call_target="tpu_custom_call" | custom-call | tf_op jit(solution)/shard_map/adafactor/pallas_call | solution.py:356
  83.9 0.7 copy.11
  84.6 0.5 copy.12
  85.1 0.6 copy.13
Async XLA Ops:
  0.6 1.6 %copy-start = (bf16[1024,1024]{1,0:T(8,128)(2,1)S(1)}, bf16[1024,1024]{1,0:T(8,128)(2,1)}, u32[]{:S(2)}) copy-start(bf16[1024,1024]{1,0:T(8,128)(2,1)} %x_hbm.1) | copy-start | bytes 6291460
  2.2 1.6 %copy-start.1 = (bf16[1024,1024]{1,0:T(8,128)(2,1)S(1)}, bf16[1024,1024]{1,0:T(8,128)(2,1)}, u32[]{:S(2)}) copy-start(bf16[1024,1024]{1,0:T(8,128)(2,1)} %c_hbm.1) | copy-start | bytes 6291460
  3.8 0.7 copy-start.2
  4.5 0.7 copy-start.3
  5.2 0.7 copy-start.4

commit v2 on v1

v2 whole, which is shorter than its diff:
```python
import functools

import jax
import jax.numpy as jnp
from jax import lax
from jax.experimental import pallas as pl
from jax.experimental.pallas import tpu as pltpu
from jax.sharding import PartitionSpec as P

MESH = pl.DeviceIdType.MESH
F32 = jnp.float32

D = 4096
F = 4096
DECAY = 0.975
EPS = 1e-30
CLIP = 1.0

NZ, NROW, NCOL, NCUT = 16, 4, 4, 2
N8 = NROW * NCUT
N32 = NCOL * N8
ROWS = 64
HALF = 32
WIDE = 1024


def make_chunks(cfg):
    zf, zs, yk = cfg["zf"], cfg["zs"], cfg["ys"]
    z, y = [], []
    for theirs in (1, 0):
        for q in range(zs):
            z.append((0, theirs, 0, HALF, q * (zf // zs), zf // zs, (1 - theirs + q) % 2))
    yw = (WIDE - zf) // yk
    for q in range(yk):
        for r in range(2):
            y.append((1, 0, r * 16, 16, zf + q * yw, yw, (r + q) % 2))
    return z, y


def kernel(cfg, *refs):
    zc, yc = make_chunks(cfg)
    chunks = zc + yc
    nch = len(chunks)
    zf = cfg["zf"]
    (x_hbm, c_hbm, gain_hbm, rprev_hbm, cprev_hbm, upd_ref, rmom_ref, cmom_ref,
     x_ref, c_ref, gain_ref, rprev_ref, cprev_ref, part) = refs[:14]
    rbufs = refs[14:14 + nch]
    (ybuf, zx_src, zx_dst, gfull, rr, rx_src, rx_dst, ab_src, ab, zab, fin,
     in_sem, ssem, rsem, ys, yr, zxs, zxr, gs, gr, rs, rrs, rxs, rxr, abs_, abr, zs, zr, fs, fr,
     ) = refs[14 + nch:]
    d = lax.axis_index("dp")
    c = lax.axis_index("cuts")
    row = lax.axis_index("row")
    col = lax.axis_index("col")
    other = 1 - c
    me8 = row * NCUT + c
    me32 = col * N8 + me8
    up = {"dp": lax.rem(d + 1, NZ)}
    down = {"dp": lax.rem(d + NZ - 1, NZ)}
    pair = {"cuts": other}

    def peer8(k):
        e = lax.rem(me8 + k, N8)
        return e, {"row": e // NCUT, "cuts": lax.rem(e, NCUT)}

    def remote(src, dst, s, r, dev):
        return pltpu.make_async_remote_copy(
            src_ref=src, dst_ref=dst, send_sem=s, recv_sem=r,
            device_id=dev, device_id_type=MESH,
        )

    barrier = pltpu.get_barrier_semaphore()

    def greet(dev):
        pl.semaphore_signal(barrier, inc=1, device_id=dev, device_id_type=MESH)

    def upper(j):
        return lax.rem(j + d, 2)

    def block(j):
        return lax.rem(d // 2 + 12 + (1 - 2 * upper(j)) * ((j + 1) // 2), 8)

    def x_load(j):
        at = pl.ds(pl.multiple_of(block(j) * 128, 128), 128)
        return pltpu.make_async_copy(x_hbm.at[:, at], x_ref.at[:, at], in_sem.at[j])

    c_loads = [
        pltpu.make_async_copy(c_hbm.at[pl.ds(n * 256, 256)], c_ref.at[pl.ds(n * 256, 256)], in_sem.at[8 + n])
        for n in range(4)
    ]
    small_loads = [
        pltpu.make_async_copy(a, b, in_sem.at[12 + n])
        for n, (a, b) in enumerate([
            (gain_hbm, gain_ref), (rprev_hbm, rprev_ref), (cprev_hbm, cprev_ref),
        ])
    ]
    x_load(0).start()
    for load in c_loads:
        load.start()
    for j in range(1, 8):
        x_load(j).start()
    for load in small_loads:
        load.start()
    greet(up)
    greet(down)
    for k in range(1, N8):
        greet(peer8(k)[1])
    for k in range(1, NCOL):
        greet({"col": lax.rem(col + k, NCOL)})
    for load in c_loads:
        load.wait()

    def product(j):
        at = pl.ds(pl.multiple_of(block(j) * 128, 128), 128)
        x_load(j).wait()
        part[at, :] = lax.dot_general(
            x_ref[:, at], c_ref[...], (((0,), (0,)), ((), ())),
            preferred_element_type=F32,
        )

    def y_copy(e):
        rows_ = pl.ds(pl.multiple_of(e * ROWS + other * HALF, HALF), HALF)
        return remote(part.at[rows_, pl.ds(zf, WIDE - zf)], ybuf.at[e], ys.at[e], yr.at[e], pair)

    def y_send(j):
        p = block(j)
        y_copy(2 * p + upper(j)).start()
        y_copy(2 * p + 1 - upper(j)).start()

    def first(j, _):
        product(j)
        return 0

    def later(j, _):
        product(j)
        y_send(j)
        return 0

    def own(e, chunk):
        _, theirs, r0, nr, c0, w, _ = chunk
        h = other if theirs else c
        return part.at[pl.ds(pl.multiple_of(e * ROWS + h * HALF + r0, nr), nr), pl.ds(c0, w)]

    def dest(direction, distance):
        return lax.rem(d + (NZ - distance if direction else distance), NZ)

    def hop(direction, n, i, src):
        ch = direction * nch + n
        return remote(
            src, rbufs[n].at[direction, i], ssem.at[ch, i], rsem.at[ch, i],
            {"dp": dest(direction, 1)},
        )

    def begin(direction, n, i):
        hop(direction, n, i, own(dest(direction, 8 - i), chunks[n])).start()

    def forward(direction, n, i):
        slot = rbufs[n].at[direction, i - 1]
        hop(direction, n, i - 1, slot).wait_recv()
        slot[...] += own(dest(direction, 8 - i), chunks[n])[...]
        hop(direction, n, i, slot).start()

    def y_add(e):
        y_copy(e).wait_recv()
        rows_ = pl.ds(pl.multiple_of(e * ROWS + c * HALF, HALF), HALF)
        part[rows_, pl.ds(zf, WIDE - zf)] += ybuf[e]

    zn = range(len(zc))
    yn = range(len(zc), nch)

    def start0(which_n):
        for n in which_n:
            begin(chunks[n][6], n, 0)

    def start1(which_n):
        for n in which_n:
            begin(1 - chunks[n][6], n, 1)

    def second(which_n):
        for n in which_n:
            forward(chunks[n][6], n, 1)

    def z_step(i):
        for n in zn:
            for direction in (0, 1):
                forward(direction, n, i)

    def y_step(i):
        for direction in (0, 1):
            y_add(dest(direction, 8 - i))
        for n in yn:
            for direction in (0, 1):
                forward(direction, n, i)

    product(0)
    pl.semaphore_wait(barrier, 2 + (N8 - 1) + (NCOL - 1))
    start0(zn)
    y_send(0)

    def fill(j, _):
        product(j)
        y_send(j)

        @pl.when(j == 1)
        def _():
            start1(zn)

        @pl.when(j == 5)
        def _():
            second(zn)

        return 0

    lax.fori_loop(1, 8, fill, 0)
    for load in small_loads:
        load.wait()
    y_add(dest(0, 8))
    start0(yn)
    z_step(2)
    for direction in (0, 1):
        y_add(dest(direction, 7))
    start1(yn)
    second(yn)

    def steps(i, _):
        z_step(i)
        y_step(i - 1)
        return 0

    lax.fori_loop(3, 8, steps, 0)

    def collect(n):
        for direction in (0, 1):
            hop(direction, n, 7, rbufs[n].at[direction, 7]).wait_recv()
        return own(d, chunks[n])[...] + rbufs[n][0, 7] + rbufs[n][1, 7]

    for n in zn:
        _, theirs, r0, nr, c0, w, _ = chunks[n]
        if theirs:
            zx_src[:, pl.ds(c0, w)] = collect(n)
    zx = remote(zx_src, zx_dst, zxs, zxr, pair)
    zx.start()
    y_step(7)
    y_add(d)

    lane = lax.broadcasted_iota(jnp.int32, (HALF, WIDE), 1)
    sub = lax.broadcasted_iota(jnp.int32, (HALF, WIDE), 0)
    gain = jnp.sum(
        jnp.where(lane == sub + d * ROWS + c * HALF, gain_ref[...], 0.0), axis=1, keepdims=True
    )
    mine = pl.ds(pl.multiple_of(c * HALF, HALF), HALF)
    for n in zn:
        _, theirs, r0, nr, c0, w, _ = chunks[n]
        if not theirs:
            gfull[mine, pl.ds(c0, w)] = collect(n)
    zx.wait_recv()
    gfull[mine, pl.ds(0, zf)] += zx_dst[...]
    for n in yn:
        _, theirs, r0, nr, c0, w, _ = chunks[n]
        gfull[pl.ds(pl.multiple_of(c * HALF + r0, nr), nr), pl.ds(c0, w)] = collect(n)
    g = gfull[mine, :] * gain
    gfull[mine, :] = g
    g_copy = remote(gfull.at[mine], gfull.at[mine], gs, gr, pair)

    lane1 = lax.broadcasted_iota(jnp.int32, (HALF, 128), 1)
    sub1 = lax.broadcasted_iota(jnp.int32, (HALF, 128), 0)
    diag = lane1 == sub1 + c * HALF
    sq = g * g
    rsum = jnp.sum(sq, axis=1, keepdims=True)
    rr[col] = jnp.sum(jnp.where(diag, rsum, 0.0), axis=0, keepdims=True)
    rcopies = []
    for k in range(1, NCOL):
        to = lax.rem(col + k, NCOL)
        cp = remote(rr.at[col], rr.at[col], rs.at[k], rrs.at[col], {"col": to})
        cp.start()
        rcopies.append(cp)
    g_copy.start()
    asum = jnp.sum(sq, axis=0, keepdims=True)
    for e in range(N8):
        ab_src[e, :, pl.ds(0, 128)] = asum[:, e * 128:(e + 1) * 128]
    for k in range(1, NCOL):
        frm = lax.rem(col + k, NCOL)
        remote(rr.at[frm], rr.at[frm], rs.at[k], rrs.at[frm], {"col": frm}).wait_recv()
    total = rr[0] + rr[1] + rr[2] + rr[3]
    lane_r = lax.broadcasted_iota(jnp.int32, (1, 128), 1)
    in_half = (lane_r >= c * HALF) & (lane_r < c * HALF + HALF)
    rprev = jnp.concatenate([rprev_ref[...], rprev_ref[...]], axis=1)
    rmom = DECAY * rprev + (1.0 - DECAY) * (total / F + EPS)
    rmom = jnp.where(in_half, rmom, 0.0)
    rcol = jnp.sum(jnp.where(diag, rmom, 0.0), axis=1, keepdims=True)
    bsum = jnp.sum(sq * (1.0 / rcol), axis=0, keepdims=True)
    for e in range(N8):
        ab_src[e, :, pl.ds(128, 128)] = bsum[:, e * 128:(e + 1) * 128]

    acopies = []
    for k in range(1, N8):
        e, dev = peer8(k)
        cp = remote(ab_src.at[e], ab.at[me8], abs_.at[k], abr.at[me8], dev)
        cp.start()
        acopies.append(cp)
    rx_src[...] = rmom
    rx = remote(rx_src, rx_dst, rxs, rxr, pair)
    rx.start()
    ab[me8] = ab_src[me8]
    for k in range(1, N8):
        e, dev = peer8(k)
        remote(ab_src.at[e], ab.at[e], abs_.at[k], abr.at[e], dev).wait_recv()
    acc = ab[0]
    for e in range(1, N8):
        acc = acc + ab[e]

    zab[d] = acc
    zcopies = []
    order = [8] + [k for m in range(7, 0, -1) for k in (m, 16 - m)]
    for k in order:
        to = lax.rem(d + k, NZ)
        cp = remote(zab.at[d], zab.at[d], zs.at[k], zr.at[d], {"dp": to})
        cp.start()
        zcopies.append(cp)
    cprev = cprev_ref[:, pl.ds(pl.multiple_of(me8 * 128, 128), 128)]
    for k in reversed(order):
        frm = lax.rem(d + k, NZ)
        remote(zab.at[frm], zab.at[frm], zs.at[k], zr.at[frm], {"dp": frm}).wait_recv()
    acc = zab[0]
    for e in range(1, NZ):
        acc = acc + zab[e]
    cmom = DECAY * cprev + (1.0 - DECAY) * (acc[:, 0:128] / D + EPS)
    fin[me32, :, pl.ds(0, 128)] = cmom
    fin[me32, :, pl.ds(128, 128)] = acc[:, 128:256] / cmom

    def plane(k):
        e = lax.rem(me32 + k, N32)
        return e, {
            "col": e // N8,
            "row": lax.rem(e, N8) // NCUT,
            "cuts": lax.rem(e, NCUT),
        }

    fcopies = []
    for k in range(1, N32):
        _, dev = plane(k)
        cp = remote(fin.at[me32], fin.at[me32], fs.at[k], fr.at[me32], dev)
        cp.start()
        fcopies.append(cp)

    rx.wait_recv()
    rfull = rmom + rx_dst[...]
    rmom_ref[...] = rfull[:, 0:ROWS]
    lane2 = lax.broadcasted_iota(jnp.int32, (ROWS, 128), 1)
    sub2 = lax.broadcasted_iota(jnp.int32, (ROWS, 128), 0)
    rscale = lax.rsqrt(jnp.sum(jnp.where(lane2 == sub2, rfull, 0.0), axis=1, keepdims=True))
    g_copy.wait_recv()

    for n in range(nch):
        for direction in (0, 1):
            lo = 0 if direction == chunks[n][6] else 1

            def drain(i, _, direction=direction, n=n):
                hop(direction, n, i, rbufs[n].at[direction, i]).wait_send()
                return 0

            lax.fori_loop(lo, 8, drain, 0)

    def drain_y(e, _):
        y_copy(e).wait_send()
        return 0

    lax.fori_loop(0, NZ, drain_y, 0)
    zx.wait_send()
    g_copy.wait_send()
    rx.wait_send()
    for cp in rcopies + acopies + zcopies:
        cp.wait_send()

    for k in range(1, N32):
        e, dev = plane(k)
        remote(fin.at[e], fin.at[e], fs.at[k], fr.at[e], dev).wait_recv()
    tot = fin[0, :, pl.ds(128, 128)]
    for e in range(1, N32):
        tot = tot + fin[e, :, pl.ds(128, 128)]
    ratio = jnp.sum(tot, axis=1, keepdims=True) / (D * F)
    inverse = 1.0 / jnp.maximum(1.0, jnp.sqrt(ratio) / CLIP)
    rows_scale = rscale * inverse
    for e in range(N8):
        at = pl.ds(e * 128, 128)
        cm = fin[col * N8 + e, :, pl.ds(0, 128)]
        cmom_ref[:, at] = cm
        upd_ref[:, at] = gfull[:, at] * rows_scale * lax.rsqrt(cm)
    for cp in fcopies:
        cp.wait_send()


def call(cfg, cid, name, tokens, cotangent, norm_gain, row_prev, col_prev):
    zc, yc = make_chunks(cfg)
    chunks = zc + yc
    nch = len(chunks)
    zf = cfg["zf"]
    vmem = pl.BlockSpec(memory_space=pltpu.VMEM)
    hbm = pl.BlockSpec(memory_space=pl.ANY)
    dma = pltpu.SemaphoreType.DMA
    bf = jnp.bfloat16
    return pl.pallas_call(
        functools.partial(kernel, cfg),
        out_shape=(
            jax.ShapeDtypeStruct((ROWS, WIDE), F32),
            jax.ShapeDtypeStruct((1, ROWS), F32),
            jax.ShapeDtypeStruct((1, WIDE), F32),
        ),
        in_specs=[hbm] * 5,
        out_specs=(vmem, vmem, vmem),
        scratch_shapes=[
            pltpu.VMEM((1024, 1024), bf),
            pltpu.VMEM((1024, 1024), bf),
            pltpu.VMEM((1, 1024), F32),
            pltpu.VMEM((1, ROWS), F32),
            pltpu.VMEM((1, WIDE), F32),
            pltpu.VMEM((1024, WIDE), F32),
        ] + [pltpu.VMEM((2, 8, ch[3], ch[5]), F32) for ch in chunks] + [
            pltpu.VMEM((NZ, HALF, WIDE - zf), F32),
            pltpu.VMEM((HALF, zf), F32),
            pltpu.VMEM((HALF, zf), F32),
            pltpu.VMEM((ROWS, WIDE), F32),
            pltpu.VMEM((NCOL, 1, 128), F32),
            pltpu.VMEM((1, 128), F32),
            pltpu.VMEM((1, 128), F32),
            pltpu.VMEM((N8, 1, 256), F32),
            pltpu.VMEM((N8, 1, 256), F32),
            pltpu.VMEM((NZ, 1, 256), F32),
            pltpu.VMEM((N32, 1, 256), F32),
            dma((15,)),
            dma((2 * nch, 8)), dma((2 * nch, 8)),
            dma((NZ,)), dma((NZ,)),
            dma, dma, dma, dma,
            dma((NCOL,)), dma((NCOL,)),
            dma, dma,
            dma((N8,)), dma((N8,)),
            dma((NZ,)), dma((NZ,)),
            dma((N32,)), dma((N32,)),
        ],
        compiler_params=pltpu.CompilerParams(
            collective_id=cid, has_side_effects=True, vmem_limit_bytes=56 << 20
        ),
        name=name,
    )(tokens, cotangent, norm_gain[None, :], row_prev, col_prev[None, :])


def write(u, r, c, uo, ro, co, sem):
    copies = [
        pltpu.make_async_copy(a, b, sem.at[n]) for n, (a, b) in enumerate([(u, uo), (r, ro), (c, co)])
    ]
    for cp in copies:
        cp.start()
    for cp in copies:
        cp.wait()


def body(tokens, cotangent, norm_gain, row_prev, col_prev):
    vmem = pl.BlockSpec(memory_space=pltpu.VMEM)
    hbm = pl.BlockSpec(memory_space=pl.ANY)
    u, r, c = call(CFG, 0, "adafactor", tokens, cotangent, norm_gain, row_prev, col_prev)
    u, r, c = pl.pallas_call(
        write,
        out_shape=tuple(jax.ShapeDtypeStruct(a.shape, F32) for a in (u, r, c)),
        in_specs=[vmem] * 3,
        out_specs=(hbm,) * 3,
        scratch_shapes=[pltpu.SemaphoreType.DMA((3,))],
        name="write",
    )(u, r, c)
    return u[None], r, c[0]


CFG = {"zf": 512, "zs": 1, "ys": 1}


def solution(mesh):
    return jax.shard_map(
        body,
        mesh=mesh,
        in_specs=(
            P(("cuts", "dp"), "row"),
            P(("cuts", "dp"), "col"),
            P("row"),
            P("row", "dp"),
            P("col"),
        ),
        out_specs=(P("row", "dp", "col"), P("row", "dp"), P("col")),
        check_vma=False,
    )
```

time: 85.9 us -> 76.5 us (0.89)
  local copies, waits for them, and re-layouts: 7.01 us -> 0 us
  Pallas kernels: 78 us -> 75.8 us
    unnamed x13 -> x0, local copies, waits for them, and re-layouts: 7.01 us -> none
    pallas_call x1 -> x2, Pallas kernels: 78 us -> 75.8 us  [the longest x1 74.1 us: call(): pl.pallas_call(functools.partial(kernel, cfg), out_shape=(jax.ShapeDtypeS...]
where the time goes in v2:
time: 76.5 us; the launch traced here: 76.4 us
  Pallas kernels  75.8 us (99%)
    pallas_call x1, Pallas kernels, call(): pl.pallas_call(functools.partial(kernel, cfg), out_shape=(jax.ShapeDtypeS...  74.1 us
    pallas_call x1, Pallas kernels, body(): pl.pallas_call(write, out_shape=tuple((jax.ShapeDtypeStruct(a.shape, F32)...  1.69 us

profile of v2, /device:TPU:1, one launch (start us, length us, event | category | flops | bytes accessed | tf_op | source)
XLA Modules:
  0.0 76.4 jit_solution(16535423798232645791)
XLA Ops:
  0.6 74.1 %adafactor.1 = (f32[64,1024]{1,0:T(8,128)}, f32[1,64]{1,0:T(1,128)}, f32[1,1024]{1,0:T(1,128)}) custom-call(bf16[1024,1024]{1,0:T(8,128)(2,1)} %refs_0_.1, bf16[1024,1024]{1,0:T(8,128)(2,1)} %refs_1_.1, f32[1,1024]{1,0:T(1,128)} %bitcast.4, f32[1,64]{1,0:T(1,128)} %refs_3_.1, f32[1,1024]{1,0:T(1,128)} %bitcast.5), custom_call_target="tpu_custom_call" | custom-call | tf_op jit(solution)/shard_map/adafactor/pallas_call | solution.py:402
  74.7 1.7 %write.1 = (f32[64,1024]{1,0:T(8,128)}, f32[1,64]{1,0:T(1,128)}, f32[1,1024]{1,0:T(1,128)}) custom-call(f32[64,1024]{1,0:T(8,128)} %get-tuple-element.9.u, f32[1,64]{1,0:T(1,128)} %get-tuple-element.10.r, f32[1,1024]{1,0:T(1,128)} %get-tuple-element.11.c), custom_call_target="tpu_custom_call" | custom-call | tf_op jit(solution)/shard_map/write/pallas_call | solution.py:461

commit v3 on v2

--- a/solution.py
+++ b/solution.py
@@ -59,9 +59,18 @@
     down = {"dp": lax.rem(d + NZ - 1, NZ)}
     pair = {"cuts": other}
 
-    def peer8(k):
-        e = lax.rem(me8 + k, N8)
-        return e, {"row": e // NCUT, "cuts": lax.rem(e, NCUT)}
+    rows4 = [lax.rem(row + k, NROW) for k in range(NROW)]
+    cols4 = [lax.rem(col + k, NCOL) for k in range(NCOL)]
+    cuts2 = [c, other]
+
+    group = [
+        (rows4[a] * NCUT + cuts2[b], {"row": rows4[a], "cuts": cuts2[b]})
+        for a in range(NROW) for b in range(NCUT) if a or b
+    ]
+    plane = [
+        (cols4[k] * N8 + rows4[a] * NCUT + cuts2[b], {"col": cols4[k], "row": rows4[a], "cuts": cuts2[b]})
+        for k in (2, 1, 3, 0) for a in (2, 1, 3, 0) for b in (1, 0) if k or a or b
+    ]
 
     def remote(src, dst, s, r, dev):
         return pltpu.make_async_remote_copy(
@@ -97,18 +106,20 @@
     x_load(0).start()
     for load in c_loads:
         load.start()
-    for j in range(1, 8):
+    for j in range(1, 4):
+        x_load(j).start()
+    greet(up)
+    greet(down)
+    for _, dev in group:
+        greet(dev)
+    for k in range(1, NCOL):
+        greet({"col": cols4[k]})
+    for load in c_loads:
+        load.wait()
+    for j in range(4, 8):
         x_load(j).start()
     for load in small_loads:
         load.start()
-    greet(up)
-    greet(down)
-    for k in range(1, N8):
-        greet(peer8(k)[1])
-    for k in range(1, NCOL):
-        greet({"col": lax.rem(col + k, NCOL)})
-    for load in c_loads:
-        load.wait()
 
     def product(j):
         at = pl.ds(pl.multiple_of(block(j) * 128, 128), 128)
@@ -181,37 +192,38 @@
             forward(chunks[n][6], n, 1)
 
     def z_step(i):
-        for n in zn:
-            for direction in (0, 1):
-                forward(direction, n, i)
+        for ahead in (1, 0):
+            for n in zn:
+                forward(chunks[n][6] ^ ahead, n, i)
 
     def y_step(i):
         for direction in (0, 1):
             y_add(dest(direction, 8 - i))
-        for n in yn:
-            for direction in (0, 1):
-                forward(direction, n, i)
-
-    product(0)
-    pl.semaphore_wait(barrier, 2 + (N8 - 1) + (NCOL - 1))
-    start0(zn)
-    y_send(0)
+        for ahead in (1, 0):
+            for n in yn:
+                forward(chunks[n][6] ^ ahead, n, i)
 
     def fill(j, _):
         product(j)
+
+        @pl.when(j == 0)
+        def _():
+            pl.semaphore_wait(barrier, 2 + (N8 - 1) + (NCOL - 1))
+            start0(zn)
+
         y_send(j)
 
         @pl.when(j == 1)
         def _():
             start1(zn)
 
-        @pl.when(j == 5)
+        @pl.when(j == 6)
         def _():
             second(zn)
 
         return 0
 
-    lax.fori_loop(1, 8, fill, 0)
+    lax.fori_loop(0, 8, fill, 0)
     for load in small_loads:
         load.wait()
     y_add(dest(0, 8))
@@ -270,7 +282,7 @@
     rr[col] = jnp.sum(jnp.where(diag, rsum, 0.0), axis=0, keepdims=True)
     rcopies = []
     for k in range(1, NCOL):
-        to = lax.rem(col + k, NCOL)
+        to = cols4[k]
         cp = remote(rr.at[col], rr.at[col], rs.at[k], rrs.at[col], {"col": to})
         cp.start()
         rcopies.append(cp)
@@ -279,7 +291,7 @@
     for e in range(N8):
         ab_src[e, :, pl.ds(0, 128)] = asum[:, e * 128:(e + 1) * 128]
     for k in range(1, NCOL):
-        frm = lax.rem(col + k, NCOL)
+        frm = cols4[k]
         remote(rr.at[frm], rr.at[frm], rs.at[k], rrs.at[frm], {"col": frm}).wait_recv()
     total = rr[0] + rr[1] + rr[2] + rr[3]
     lane_r = lax.broadcasted_iota(jnp.int32, (1, 128), 1)
@@ -293,8 +305,7 @@
         ab_src[e, :, pl.ds(128, 128)] = bsum[:, e * 128:(e + 1) * 128]
 
     acopies = []
-    for k in range(1, N8):
-        e, dev = peer8(k)
+    for k, (e, dev) in enumerate(group):
         cp = remote(ab_src.at[e], ab.at[me8], abs_.at[k], abr.at[me8], dev)
         cp.start()
         acopies.append(cp)
@@ -302,8 +313,7 @@
     rx = remote(rx_src, rx_dst, rxs, rxr, pair)
     rx.start()
     ab[me8] = ab_src[me8]
-    for k in range(1, N8):
-        e, dev = peer8(k)
+    for k, (e, dev) in enumerate(group):
         remote(ab_src.at[e], ab.at[e], abs_.at[k], abr.at[e], dev).wait_recv()
     acc = ab[0]
     for e in range(1, N8):
@@ -328,17 +338,8 @@
     fin[me32, :, pl.ds(0, 128)] = cmom
     fin[me32, :, pl.ds(128, 128)] = acc[:, 128:256] / cmom
 
-    def plane(k):
-        e = lax.rem(me32 + k, N32)
-        return e, {
-            "col": e // N8,
-            "row": lax.rem(e, N8) // NCUT,
-            "cuts": lax.rem(e, NCUT),
-        }
-
     fcopies = []
-    for k in range(1, N32):
-        _, dev = plane(k)
+    for k, (_, dev) in enumerate(plane):
         cp = remote(fin.at[me32], fin.at[me32], fs.at[k], fr.at[me32], dev)
         cp.start()
         fcopies.append(cp)
@@ -372,8 +373,7 @@
     for cp in rcopies + acopies + zcopies:
         cp.wait_send()
 
-    for k in range(1, N32):
-        e, dev = plane(k)
+    for k, (e, dev) in enumerate(plane):
         remote(fin.at[e], fin.at[e], fs.at[k], fr.at[e], dev).wait_recv()
     tot = fin[0, :, pl.ds(128, 128)]
     for e in range(1, N32):
@@ -396,7 +396,7 @@
     nch = len(chunks)
     zf = cfg["zf"]
     vmem = pl.BlockSpec(memory_space=pltpu.VMEM)
-    hbm = pl.BlockSpec(memory_space=pl.ANY)
+    hbm = pl.BlockSpec(memory_space=pltpu.HBM)
     dma = pltpu.SemaphoreType.DMA
     bf = jnp.bfloat16
     return pl.pallas_call(
@@ -461,15 +461,16 @@
     u, r, c = pl.pallas_call(
         write,
         out_shape=tuple(jax.ShapeDtypeStruct(a.shape, F32) for a in (u, r, c)),
-        in_specs=[vmem] * 3,
+        in_specs=[hbm] * 3,
         out_specs=(hbm,) * 3,
         scratch_shapes=[pltpu.SemaphoreType.DMA((3,))],
+        compiler_params=pltpu.CompilerParams(vmem_limit_bytes=60 << 20),
         name="write",
     )(u, r, c)
     return u[None], r, c[0]
 
 
-CFG = {"zf": 512, "zs": 1, "ys": 1}
+CFG = {"zf": 384, "zs": 1, "ys": 1}
 
 
 def solution(mesh):

time: 76.5 us -> 82.7 us (1.081)
  Pallas kernels: 75.8 us -> 82 us
    pallas_call x1, Pallas kernels: 1.69 us -> 9.21 us  [body(): pl.pallas_call(write, out_shape=tuple((jax.ShapeDtypeStruct(a.shape, F32)...]
    pallas_call x1, Pallas kernels: 74.1 us -> 72.7 us  [call(): pl.pallas_call(functools.partial(kernel, cfg), out_shape=(jax.ShapeDtypeS...]
where the time goes in v3:
time: 82.7 us; the launch traced here: 82.6 us
  Pallas kernels  82 us (99%)
    pallas_call x1, Pallas kernels, call(): pl.pallas_call(functools.partial(kernel, cfg), out_shape=(jax.ShapeDtypeS...  72.7 us
    pallas_call x1, Pallas kernels, body(): pl.pallas_call(write, out_shape=tuple((jax.ShapeDtypeStruct(a.shape, F32)...  9.21 us

profile of v3, /device:TPU:1, one launch (start us, length us, event | category | flops | bytes accessed | tf_op | source)
XLA Modules:
  0.0 82.6 jit_solution(793612990906451473)
XLA Ops:
  0.6 72.7 %adafactor.1 = (f32[64,1024]{1,0:T(8,128)}, f32[1,64]{1,0:T(1,128)}, f32[1,1024]{1,0:T(1,128)}) custom-call(bf16[1024,1024]{1,0:T(8,128)(2,1)} %refs_0_.1, bf16[1024,1024]{1,0:T(8,128)(2,1)} %refs_1_.1, f32[1,1024]{1,0:T(1,128)} %bitcast.4, f32[1,64]{1,0:T(1,128)} %refs_3_.1, f32[1,1024]{1,0:T(1,128)} %bitcast.5), custom_call_target="tpu_custom_call" | custom-call | tf_op jit(solution)/shard_map/adafactor/pallas_call | solution.py:402
  73.4 9.2 %write.1 = (f32[64,1024]{1,0:T(8,128)}, f32[1,64]{1,0:T(1,128)}, f32[1,1024]{1,0:T(1,128)}) custom-call(f32[64,1024]{1,0:T(8,128)} %get-tuple-element.9.u, f32[1,64]{1,0:T(1,128)} %get-tuple-element.10.r, f32[1,1024]{1,0:T(1,128)} %get-tuple-element.11.c), custom_call_target="tpu_custom_call" | custom-call | tf_op jit(solution)/shard_map/write/pallas_call | solution.py:461

commit v4 on v3

--- a/solution.py
+++ b/solution.py
@@ -42,12 +42,13 @@
     chunks = zc + yc
     nch = len(chunks)
     zf = cfg["zf"]
-    (x_hbm, c_hbm, gain_hbm, rprev_hbm, cprev_hbm, upd_ref, rmom_ref, cmom_ref,
-     x_ref, c_ref, gain_ref, rprev_ref, cprev_ref, part) = refs[:14]
-    rbufs = refs[14:14 + nch]
+    (x_hbm, c_hbm, gain_hbm, rprev_hbm, cprev_hbm, upd_hbm, rmom_hbm, cmom_hbm,
+     upd_ref, rmom_ref, cmom_ref, out_sem,
+     x_ref, c_ref, gain_ref, rprev_ref, cprev_ref, part) = refs[:18]
+    rbufs = refs[18:18 + nch]
     (ybuf, zx_src, zx_dst, gfull, rr, rx_src, rx_dst, ab_src, ab, zab, fin,
      in_sem, ssem, rsem, ys, yr, zxs, zxr, gs, gr, rs, rrs, rxs, rxr, abs_, abr, zs, zr, fs, fr,
-     ) = refs[14 + nch:]
+     ) = refs[18 + nch:]
     d = lax.axis_index("dp")
     c = lax.axis_index("cuts")
     row = lax.axis_index("row")
@@ -347,6 +348,8 @@
     rx.wait_recv()
     rfull = rmom + rx_dst[...]
     rmom_ref[...] = rfull[:, 0:ROWS]
+    outs = [pltpu.make_async_copy(rmom_ref, rmom_hbm, out_sem.at[N8])]
+    outs[0].start()
     lane2 = lax.broadcasted_iota(jnp.int32, (ROWS, 128), 1)
     sub2 = lax.broadcasted_iota(jnp.int32, (ROWS, 128), 0)
     rscale = lax.rsqrt(jnp.sum(jnp.where(lane2 == sub2, rfull, 0.0), axis=1, keepdims=True))
@@ -386,8 +389,14 @@
         cm = fin[col * N8 + e, :, pl.ds(0, 128)]
         cmom_ref[:, at] = cm
         upd_ref[:, at] = gfull[:, at] * rows_scale * lax.rsqrt(cm)
+        outs.append(pltpu.make_async_copy(upd_ref.at[:, at], upd_hbm.at[:, at], out_sem.at[e]))
+        outs[-1].start()
+    outs.append(pltpu.make_async_copy(cmom_ref, cmom_hbm, out_sem.at[N8 + 1]))
+    outs[-1].start()
     for cp in fcopies:
         cp.wait_send()
+    for cp in outs:
+        cp.wait()
 
 
 def call(cfg, cid, name, tokens, cotangent, norm_gain, row_prev, col_prev):
@@ -395,8 +404,7 @@
     chunks = zc + yc
     nch = len(chunks)
     zf = cfg["zf"]
-    vmem = pl.BlockSpec(memory_space=pltpu.VMEM)
-    hbm = pl.BlockSpec(memory_space=pltpu.HBM)
+    hbm = pl.BlockSpec(memory_space=pl.ANY)
     dma = pltpu.SemaphoreType.DMA
     bf = jnp.bfloat16
     return pl.pallas_call(
@@ -407,8 +415,12 @@
             jax.ShapeDtypeStruct((1, WIDE), F32),
         ),
         in_specs=[hbm] * 5,
-        out_specs=(vmem, vmem, vmem),
+        out_specs=(hbm, hbm, hbm),
         scratch_shapes=[
+            pltpu.VMEM((ROWS, WIDE), F32),
+            pltpu.VMEM((1, ROWS), F32),
+            pltpu.VMEM((1, WIDE), F32),
+            dma((N8 + 2,)),
             pltpu.VMEM((1024, 1024), bf),
             pltpu.VMEM((1024, 1024), bf),
             pltpu.VMEM((1, 1024), F32),
@@ -444,18 +456,22 @@
     )(tokens, cotangent, norm_gain[None, :], row_prev, col_prev[None, :])
 
 
-def write(u, r, c, uo, ro, co, sem):
-    copies = [
-        pltpu.make_async_copy(a, b, sem.at[n]) for n, (a, b) in enumerate([(u, uo), (r, ro), (c, co)])
-    ]
-    for cp in copies:
+def write(u, r, c, uo, ro, co, uv, rv, cv, isem, osem):
+    pieces = 4
+    rows_ = [pl.ds(n * (ROWS // pieces), ROWS // pieces) for n in range(pieces)]
+    pairs = [(u.at[at], uv.at[at], uo.at[at]) for at in rows_] + [(r, rv, ro), (c, cv, co)]
+    ins = [pltpu.make_async_copy(a, b, isem.at[n]) for n, (a, b, _) in enumerate(pairs)]
+    outs = [pltpu.make_async_copy(b, o, osem.at[n]) for n, (_, b, o) in enumerate(pairs)]
+    for cp in ins:
         cp.start()
-    for cp in copies:
+    for a, b in zip(ins, outs):
+        a.wait()
+        b.start()
+    for cp in outs:
         cp.wait()
 
 
 def body(tokens, cotangent, norm_gain, row_prev, col_prev):
-    vmem = pl.BlockSpec(memory_space=pltpu.VMEM)
     hbm = pl.BlockSpec(memory_space=pl.ANY)
     u, r, c = call(CFG, 0, "adafactor", tokens, cotangent, norm_gain, row_prev, col_prev)
     u, r, c = pl.pallas_call(
@@ -463,7 +479,13 @@
         out_shape=tuple(jax.ShapeDtypeStruct(a.shape, F32) for a in (u, r, c)),
         in_specs=[hbm] * 3,
         out_specs=(hbm,) * 3,
-        scratch_shapes=[pltpu.SemaphoreType.DMA((3,))],
+        scratch_shapes=[
+            pltpu.VMEM((ROWS, WIDE), F32),
+            pltpu.VMEM((1, ROWS), F32),
+            pltpu.VMEM((1, WIDE), F32),
+            pltpu.SemaphoreType.DMA((6,)),
+            pltpu.SemaphoreType.DMA((6,)),
+        ],
         compiler_params=pltpu.CompilerParams(vmem_limit_bytes=60 << 20),
         name="write",
     )(u, r, c)

time: 82.7 us -> 74.9 us (0.906)
  Pallas kernels: 82 us -> 74.1 us
    pallas_call x1, Pallas kernels: 9.21 us -> 1.67 us  [body(): pl.pallas_call(write, out_shape=tuple((jax.ShapeDtypeStruct(a.shape, F32)...]
where the time goes in v4:
time: 74.9 us; the launch traced here: 74.7 us
  Pallas kernels  74.1 us (99%)
    pallas_call x1, Pallas kernels, call(): pl.pallas_call(functools.partial(kernel, cfg), out_shape=(jax.ShapeDtypeS...  72.4 us
    pallas_call x1, Pallas kernels, body(): pl.pallas_call(write, out_shape=tuple((jax.ShapeDtypeStruct(a.shape, F32)...  1.67 us

profile of v4, /device:TPU:1, one launch (start us, length us, event | category | flops | bytes accessed | tf_op | source)
XLA Modules:
  0.0 74.7 jit_solution(15258623253658585801)
XLA Ops:
  0.6 72.4 %adafactor.1 = (f32[64,1024]{1,0:T(8,128)}, f32[1,64]{1,0:T(1,128)}, f32[1,1024]{1,0:T(1,128)}) custom-call(bf16[1024,1024]{1,0:T(8,128)(2,1)} %refs_0_.1, bf16[1024,1024]{1,0:T(8,128)(2,1)} %refs_1_.1, f32[1,1024]{1,0:T(1,128)} %bitcast.4, f32[1,64]{1,0:T(1,128)} %refs_3_.1, f32[1,1024]{1,0:T(1,128)} %bitcast.5), custom_call_target="tpu_custom_call" | custom-call | tf_op jit(solution)/shard_map/adafactor/pallas_call | solution.py:410
  73.0 1.7 %write.1 = (f32[64,1024]{1,0:T(8,128)}, f32[1,64]{1,0:T(1,128)}, f32[1,1024]{1,0:T(1,128)}) custom-call(f32[64,1024]{1,0:T(8,128)} %get-tuple-element.9.u, f32[1,64]{1,0:T(1,128)} %get-tuple-element.10.r, f32[1,1024]{1,0:T(1,128)} %get-tuple-element.11.c), custom_call_target="tpu_custom_call" | custom-call | tf_op jit(solution)/shard_map/write/pallas_call | solution.py:477

commit v5 on v4

--- a/solution.py
+++ b/solution.py
@@ -328,6 +328,38 @@
         cp = remote(zab.at[d], zab.at[d], zs.at[k], zr.at[d], {"dp": to})
         cp.start()
         zcopies.append(cp)
+    rx.wait_recv()
+    rfull = rmom + rx_dst[...]
+    rmom_ref[...] = rfull[:, 0:ROWS]
+    outs = [pltpu.make_async_copy(rmom_ref, rmom_hbm, out_sem.at[N8])]
+    outs[0].start()
+    lane2 = lax.broadcasted_iota(jnp.int32, (ROWS, 128), 1)
+    sub2 = lax.broadcasted_iota(jnp.int32, (ROWS, 128), 0)
+    rscale = lax.rsqrt(jnp.sum(jnp.where(lane2 == sub2, rfull, 0.0), axis=1, keepdims=True))
+    g_copy.wait_recv()
+    upd_ref[...] = gfull[...] * rscale
+
+    for n in range(nch):
+        for direction in (0, 1):
+            lo = 0 if direction == chunks[n][6] else 1
+
+            def drain(i, _, direction=direction, n=n):
+                hop(direction, n, i, rbufs[n].at[direction, i]).wait_send()
+                return 0
+
+            lax.fori_loop(lo, 8, drain, 0)
+
+    def drain_y(e, _):
+        y_copy(e).wait_send()
+        return 0
+
+    lax.fori_loop(0, NZ, drain_y, 0)
+    zx.wait_send()
+    g_copy.wait_send()
+    rx.wait_send()
+    for cp in rcopies + acopies:
+        cp.wait_send()
+
     cprev = cprev_ref[:, pl.ds(pl.multiple_of(me8 * 128, 128), 128)]
     for k in reversed(order):
         frm = lax.rem(d + k, NZ)
@@ -345,37 +377,6 @@
         cp.start()
         fcopies.append(cp)
 
-    rx.wait_recv()
-    rfull = rmom + rx_dst[...]
-    rmom_ref[...] = rfull[:, 0:ROWS]
-    outs = [pltpu.make_async_copy(rmom_ref, rmom_hbm, out_sem.at[N8])]
-    outs[0].start()
-    lane2 = lax.broadcasted_iota(jnp.int32, (ROWS, 128), 1)
-    sub2 = lax.broadcasted_iota(jnp.int32, (ROWS, 128), 0)
-    rscale = lax.rsqrt(jnp.sum(jnp.where(lane2 == sub2, rfull, 0.0), axis=1, keepdims=True))
-    g_copy.wait_recv()
-
-    for n in range(nch):
-        for direction in (0, 1):
-            lo = 0 if direction == chunks[n][6] else 1
-
-            def drain(i, _, direction=direction, n=n):
-                hop(direction, n, i, rbufs[n].at[direction, i]).wait_send()
-                return 0
-
-            lax.fori_loop(lo, 8, drain, 0)
-
-    def drain_y(e, _):
-        y_copy(e).wait_send()
-        return 0
-
-    lax.fori_loop(0, NZ, drain_y, 0)
-    zx.wait_send()
-    g_copy.wait_send()
-    rx.wait_send()
-    for cp in rcopies + acopies + zcopies:
-        cp.wait_send()
-
     for k, (e, dev) in enumerate(plane):
         remote(fin.at[e], fin.at[e], fs.at[k], fr.at[e], dev).wait_recv()
     tot = fin[0, :, pl.ds(128, 128)]
@@ -383,17 +384,16 @@
         tot = tot + fin[e, :, pl.ds(128, 128)]
     ratio = jnp.sum(tot, axis=1, keepdims=True) / (D * F)
     inverse = 1.0 / jnp.maximum(1.0, jnp.sqrt(ratio) / CLIP)
-    rows_scale = rscale * inverse
     for e in range(N8):
         at = pl.ds(e * 128, 128)
         cm = fin[col * N8 + e, :, pl.ds(0, 128)]
         cmom_ref[:, at] = cm
-        upd_ref[:, at] = gfull[:, at] * rows_scale * lax.rsqrt(cm)
+        upd_ref[:, at] = upd_ref[:, at] * (lax.rsqrt(cm) * inverse)
         outs.append(pltpu.make_async_copy(upd_ref.at[:, at], upd_hbm.at[:, at], out_sem.at[e]))
         outs[-1].start()
     outs.append(pltpu.make_async_copy(cmom_ref, cmom_hbm, out_sem.at[N8 + 1]))
     outs[-1].start()
-    for cp in fcopies:
+    for cp in zcopies + fcopies:
         cp.wait_send()
     for cp in outs:
         cp.wait()

time: 74.9 us -> 74.9 us (level)
  no operation moved by 1% of the time
where the time goes in v5:
time: 74.9 us; the launch traced here: 74.7 us
  Pallas kernels  74.1 us (99%)
    pallas_call x1, Pallas kernels, call(): pl.pallas_call(functools.partial(kernel, cfg), out_shape=(jax.ShapeDtypeS...  72.4 us
    pallas_call x1, Pallas kernels, body(): pl.pallas_call(write, out_shape=tuple((jax.ShapeDtypeStruct(a.shape, F32)...  1.67 us

profile of v5, /device:TPU:1, one launch (start us, length us, event | category | flops | bytes accessed | tf_op | source)
XLA Modules:
  0.0 74.7 jit_solution(2386118988339291239)
XLA Ops:
  0.6 72.4 %adafactor.1 = (f32[64,1024]{1,0:T(8,128)}, f32[1,64]{1,0:T(1,128)}, f32[1,1024]{1,0:T(1,128)}) custom-call(bf16[1024,1024]{1,0:T(8,128)(2,1)} %refs_0_.1, bf16[1024,1024]{1,0:T(8,128)(2,1)} %refs_1_.1, f32[1,1024]{1,0:T(1,128)} %bitcast.4, f32[1,64]{1,0:T(1,128)} %refs_3_.1, f32[1,1024]{1,0:T(1,128)} %bitcast.5), custom_call_target="tpu_custom_call" | custom-call | tf_op jit(solution)/shard_map/adafactor/pallas_call | solution.py:410
  73.0 1.7 %write.1 = (f32[64,1024]{1,0:T(8,128)}, f32[1,64]{1,0:T(1,128)}, f32[1,1024]{1,0:T(1,128)}) custom-call(f32[64,1024]{1,0:T(8,128)} %get-tuple-element.9.u, f32[1,64]{1,0:T(1,128)} %get-tuple-element.10.r, f32[1,1024]{1,0:T(1,128)} %get-tuple-element.11.c), custom_call_target="tpu_custom_call" | custom-call | tf_op jit(solution)/shard_map/write/pallas_call | solution.py:477

commit v6 on v4

--- a/solution.py
+++ b/solution.py
@@ -95,11 +95,11 @@
         return pltpu.make_async_copy(x_hbm.at[:, at], x_ref.at[:, at], in_sem.at[j])
 
     c_loads = [
-        pltpu.make_async_copy(c_hbm.at[pl.ds(n * 256, 256)], c_ref.at[pl.ds(n * 256, 256)], in_sem.at[8 + n])
-        for n in range(4)
+        pltpu.make_async_copy(c_hbm.at[pl.ds(n * 128, 128)], c_ref.at[pl.ds(n * 128, 128)], in_sem.at[8 + n])
+        for n in range(8)
     ]
     small_loads = [
-        pltpu.make_async_copy(a, b, in_sem.at[12 + n])
+        pltpu.make_async_copy(a, b, in_sem.at[16 + n])
         for n, (a, b) in enumerate([
             (gain_hbm, gain_ref), (rprev_hbm, rprev_ref), (cprev_hbm, cprev_ref),
         ])
@@ -107,14 +107,14 @@
     x_load(0).start()
     for load in c_loads:
         load.start()
-    for j in range(1, 4):
-        x_load(j).start()
     greet(up)
     greet(down)
     for _, dev in group:
         greet(dev)
     for k in range(1, NCOL):
         greet({"col": cols4[k]})
+    for j in range(1, 4):
+        x_load(j).start()
     for load in c_loads:
         load.wait()
     for j in range(4, 8):
@@ -439,7 +439,7 @@
             pltpu.VMEM((N8, 1, 256), F32),
             pltpu.VMEM((NZ, 1, 256), F32),
             pltpu.VMEM((N32, 1, 256), F32),
-            dma((15,)),
+            dma((19,)),
             dma((2 * nch, 8)), dma((2 * nch, 8)),
             dma((NZ,)), dma((NZ,)),
             dma, dma, dma, dma,

time: 74.9 us -> 74.6 us (level)
  no operation moved by 1% of the time
where the time goes in v6:
time: 74.6 us; the launch traced here: 74.4 us
  Pallas kernels  73.8 us (99%)
    pallas_call x1, Pallas kernels, call(): pl.pallas_call(functools.partial(kernel, cfg), out_shape=(jax.ShapeDtypeS...  72.1 us
    pallas_call x1, Pallas kernels, body(): pl.pallas_call(write, out_shape=tuple((jax.ShapeDtypeStruct(a.shape, F32)...  1.67 us

profile of v6, /device:TPU:1, one launch (start us, length us, event | category | flops | bytes accessed | tf_op | source)
XLA Modules:
  0.0 74.4 jit_solution(7009984119332685339)
XLA Ops:
  0.6 72.1 %adafactor.1 = (f32[64,1024]{1,0:T(8,128)}, f32[1,64]{1,0:T(1,128)}, f32[1,1024]{1,0:T(1,128)}) custom-call(bf16[1024,1024]{1,0:T(8,128)(2,1)} %refs_0_.1, bf16[1024,1024]{1,0:T(8,128)(2,1)} %refs_1_.1, f32[1,1024]{1,0:T(1,128)} %bitcast.4, f32[1,64]{1,0:T(1,128)} %refs_3_.1, f32[1,1024]{1,0:T(1,128)} %bitcast.5), custom_call_target="tpu_custom_call" | custom-call | tf_op jit(solution)/shard_map/adafactor/pallas_call | solution.py:410
  72.8 1.7 %write.1 = (f32[64,1024]{1,0:T(8,128)}, f32[1,64]{1,0:T(1,128)}, f32[1,1024]{1,0:T(1,128)}) custom-call(f32[64,1024]{1,0:T(8,128)} %get-tuple-element.9.u, f32[1,64]{1,0:T(1,128)} %get-tuple-element.10.r, f32[1,1024]{1,0:T(1,128)} %get-tuple-element.11.c), custom_call_target="tpu_custom_call" | custom-call | tf_op jit(solution)/shard_map/write/pallas_call | solution.py:477
